TPU v7x, 32 devices: a whole 2x2x4 slice. The times are simulated.
32 devices in a mesh: scene: 2 (over y), pulse: 4 (over z), range: 2 (over x), rep: 2 (over core).
Axes of the slice: x: 2, y: 2, z: 4, core: 2. Of those that a mesh axis runs over, the one named last changes fastest.
Arguments:
- echo: bfloat16 [8, 64, 2, 6144], P(('scene', 'pulse'), 'rep', None, 'range'), parts along dimension 0, may hold values from -6 to 6
- chirp: bfloat16 [2, 512], replicated, may hold values from -0.1875 to 0.1875
- beam_one: int32 [2, 128], replicated, may hold values from 0 to 63, as said below
- shift_one: int32 [2, 128], replicated, may hold values from -28 to 28
- frac_one: float32 [2, 128], replicated, may hold values from 0 to 1
- base_one: float32 [2, 128], replicated, may hold values from -3.140625 to 3.140625
- beam_two: int32 [2, 256], replicated, may hold values from 0 to 127, as said below
- shift_two: int32 [2, 256], replicated, may hold values from -28 to 28
- frac_two: float32 [2, 256], replicated, may hold values from 0 to 1
- base_two: float32 [2, 256], replicated, may hold values from -3.140625 to 3.140625
Outputs:
- image: bfloat16 [2, 8, 32, 2, 6144], P('rep', ('scene', 'pulse'), None, None, 'range'), parts along dimension 1
There are 2 independent parts, one for each index of `scene`. A program takes and returns all parts, laid end to end along the dimension named above; an argument that names none is the same for every part. Nothing has to cross between parts.
Inputs may be any that keep to these rules, and one draw needn't show every extreme that they name: beam_one[c, p] differs from p // 2 by at most 1 and lies in the same aligned block of 8 child beams as p // 2; the first and last parent beams read child beams 0 and 63. beam_two[c, p] differs from p // 2 by at most 1 and lies in the same aligned block of 16 child beams as p // 2; the first and last parent beams read child beams 0 and 127.
All inputs are finite; a program needn't handle non-finite values.
Results may differ from a plain program's by a relative error of at most 0.012.
Values may be sent and summed in bfloat16 or wider, within the bound.
A program may use at most 64 MiB of HBM per device.

v0:
```python
import functools
import math

import jax
import jax.numpy as jnp
from jax import lax
from jax.experimental import pallas as pl
from jax.experimental.pallas import tpu as pltpu
from jax.sharding import PartitionSpec as P

LANES = 128
GROUP = 4
LEFT = 1
RIGHT = 5
MESH = pl.DeviceIdType.MESH


def block_of(member):
    return 2 * lax.rem(member, 2) + member // 2


def gather_kernel(chirp_ref, echo_ref, out_ref, ext, toeplitz, send_sem, recv_sem, local_sem):
    chunks = echo_ref.shape[1]
    taps = chirp_ref.shape[1]
    x = lax.axis_index("range")
    last = lax.axis_size("range") - 1
    z = lax.axis_index("pulse")
    first_member = z // GROUP * GROUP
    me = lax.rem(z, GROUP)
    has_left = x > 0
    has_right = x < last

    barrier = pltpu.get_barrier_semaphore()

    def greet(dx, dz):
        pl.semaphore_signal(
            barrier,
            inc=1,
            device_id={"range": x + dx, "pulse": first_member + lax.rem(me + dz, GROUP)},
            device_id_type=MESH,
        )

    for dz in range(1, GROUP):
        greet(0, dz)

    @pl.when(has_left)
    def _():
        for dz in range(GROUP):
            greet(-1, dz)

    @pl.when(has_right)
    def _():
        for dz in range(GROUP):
            greet(1, dz)

    def copy_to(kind, dz):
        member = lax.rem(me + dz, GROUP)
        block = block_of(member)
        dx = (0, -1, 1)[kind]
        start, count = ((0, chunks), (0, RIGHT), (chunks - LEFT, LEFT))[kind]
        target = (LEFT, LEFT + chunks, 0)[kind]
        return pltpu.make_async_remote_copy(
            src_ref=echo_ref.at[block, pl.ds(start, count)],
            dst_ref=ext.at[me, pl.ds(target, count)],
            send_sem=send_sem.at[kind, dz],
            recv_sem=recv_sem.at[kind, me],
            device_id={"range": x + dx, "pulse": first_member + member},
            device_id_type=MESH,
        )

    def arrival(kind, source):
        count = (chunks, RIGHT, LEFT)[kind]
        target = (LEFT, LEFT + chunks, 0)[kind]
        return pltpu.make_async_remote_copy(
            src_ref=ext.at[source, pl.ds(target, count)],
            dst_ref=ext.at[source, pl.ds(target, count)],
            send_sem=send_sem.at[kind, 0],
            recv_sem=recv_sem.at[kind, source],
            device_id={"range": x, "pulse": z},
            device_id_type=MESH,
        )

    own = pltpu.make_async_copy(
        echo_ref.at[block_of(me)], ext.at[me, pl.ds(LEFT, chunks)], local_sem
    )
    own.start()
    waits = GROUP - 1 + GROUP * (has_left.astype(jnp.int32) + has_right.astype(jnp.int32))
    pl.semaphore_wait(barrier, waits)

    for dz in (0, 2, 1, 3):

        @pl.when(has_left)
        def _():
            copy_to(1, dz).start()

        @pl.when(has_right)
        def _():
            copy_to(2, dz).start()

    for dz in (2, 1, 3):
        copy_to(0, dz).start()

    @pl.when(jnp.logical_not(has_right))
    def _():
        ext[:, LEFT + chunks :] = jnp.zeros((GROUP, RIGHT, 16, LANES), ext.dtype)

    @pl.when(jnp.logical_not(has_left))
    def _():
        ext[:, :LEFT] = jnp.zeros((GROUP, LEFT, 16, LANES), ext.dtype)

    span = 256 + taps
    for part in range(2):
        row = jnp.concatenate(
            [chirp_ref[part : part + 1, :].astype(jnp.float32), jnp.zeros((1, 256), jnp.float32)],
            axis=1,
        )
        rows = jnp.broadcast_to(row, (256, span))
        rolled = pltpu.roll(rows, 0, 1, stride=1, stride_axis=0)
        toeplitz[256 * part : 256 * (part + 1), :] = rolled.astype(toeplitz.dtype)

    out_blocks = (chunks + 2) // 2
    left_scale = has_left.astype(jnp.float32)
    right_scale = has_right.astype(jnp.float32)

    for dz in range(GROUP):
        source = lax.rem(me + dz, GROUP)
        if dz == 0:
            own.wait()
        else:
            arrival(0, source).wait_recv()

        @pl.when(has_right)
        def _():
            arrival(1, source).wait_recv()

        @pl.when(has_left)
        def _():
            arrival(2, source).wait_recv()

        held = ext[source].reshape((LEFT + chunks + RIGHT) // 2, 2, 16, LANES)
        pieces = [
            held[u // 2 : u // 2 + out_blocks, u % 2].reshape(out_blocks * 16, LANES)
            for u in range(span // LANES)
        ]
        windows = jnp.concatenate(pieces, axis=1)
        product = lax.dot_general(
            windows, toeplitz[...], (((1,), (1,)), ((), ())), preferred_element_type=jnp.float32
        )
        for block in range(out_blocks):
            up = product[16 * block : 16 * block + 8]
            down = product[16 * block + 8 : 16 * block + 16]
            values = (up[:, :256] + down[:, 256:], down[:, :256] - up[:, 256:])
            for half in range(2):
                chunk = 2 * block + half
                for part in range(2):
                    value = values[part][:, half * LANES : (half + 1) * LANES]
                    if chunk == 0:
                        value = value * left_scale
                    if chunk == chunks + 1:
                        value = value * right_scale
                    out_ref[source, pl.ds(32 * part + chunk, 8, stride=64), :] = value

    for dz in range(GROUP):

        @pl.when(has_left)
        def _():
            copy_to(1, dz).wait_send()

        @pl.when(has_right)
        def _():
            copy_to(2, dz).wait_send()

        if dz:
            copy_to(0, dz).wait_send()


def shifted(value, distance):
    rows = value.shape[0]
    turned = pltpu.roll(value, LANES - distance, 1)
    below = pltpu.roll(turned, rows - 1, 0)
    lane = lax.broadcasted_iota(jnp.int32, value.shape, 1)
    return jnp.where(lane < LANES - distance, turned, below)


def cos_sin(angle):
    turns = angle * (1.0 / (2.0 * math.pi))
    turns = turns - jnp.round(turns)
    half = turns * math.pi
    square = half * half
    sine = jnp.full_like(half, -1.0 / math.factorial(11))
    for n in (9, 7, 5, 3, 1):
        sine = sine * square + (-1.0) ** ((n - 1) // 2) / math.factorial(n)
    sine = sine * half
    cosine = jnp.full_like(half, 1.0 / math.factorial(12))
    for n in (10, 8, 6, 4, 2, 0):
        cosine = cosine * square + (-1.0) ** (n // 2) / math.factorial(n)
    return 1.0 - 2.0 * sine * sine, 2.0 * sine * cosine


def merge_kernel(
    beam_one, shift_one, frac_one, base_one, beam_two, shift_two, frac_two, base_two, taps,
    comp_ref, out_ref, zero_taps, one_taps,
):
    count_one = beam_one.shape[1]
    count_two = beam_two.shape[1]
    rows_out = out_ref.shape[1]
    bins = rows_out * LANES
    x = lax.axis_index("range")
    bin_total = bins * lax.axis_size("range")
    first_bin = x * bins
    z = lax.axis_index("pulse")
    block = 4 * lax.axis_index("rep") + block_of(lax.rem(z, GROUP))

    def spread(index, _):
        value = comp_ref[index]
        zero_taps[0, index] = value
        for t in range(1, 4):
            zero_taps[t, index] = shifted(value, t)
        return 0

    lax.fori_loop(0, comp_ref.shape[0], spread, 0)

    def positions(rows, margin):
        row = lax.broadcasted_iota(jnp.int32, (rows, LANES), 0)
        lane = lax.broadcasted_iota(jnp.int32, (rows, LANES), 1)
        return first_bin - margin + row * LANES + lane

    def factors(base, slope, rows, ramp):
        cosine, sine = cos_sin(base + slope * ramp)
        step = jnp.full((8, LANES), slope * (8.0 * LANES / bin_total), jnp.float32)
        step_cos, step_sin = cos_sin(step)
        cosines, sines = [cosine], [sine]
        for _ in range(rows // 8 - 1):
            cosine, sine = cosine * step_cos - sine * step_sin, sine * step_cos + cosine * step_sin
            cosines.append(cosine)
            sines.append(sine)
        return jnp.concatenate(cosines, 0), jnp.concatenate(sines, 0)

    def sampled(source, index, weights, distance, rows):
        early = weights[0] * source[0, index]
        late = weights[4] * source[0, index]
        for t in range(1, 4):
            value = source[t, index]
            early = early + weights[t] * value
            late = late + weights[t + 4] * value
        return shifted(early + shifted(late, 4), distance)[:rows]

    ramp_one = positions(8, 32).astype(jnp.float32) * (1.0 / bin_total) - 0.5
    place_one = positions(32, 32)
    inside_one = (place_one >= 0) & (place_one < bin_total)

    def first_merge(i, _):
        p = block * 16 + i
        sums = [[None, None], [None, None]]
        for c in range(2):
            beam = beam_one[c, p] - block * 8
            shift = shift_one[c, p]
            slope = 0.5 * (shift.astype(jnp.float32) + frac_one[c, p])
            cosine, sine = factors(base_one[c, p], slope, 32, ramp_one)
            weights = [taps[(c * (count_one + count_two) + p) * 8 + t] for t in range(8)]
            for q in range(2):
                index = ((2 * q + c) * 8 + beam) * 2
                real = sampled(zero_taps, index, weights, shift + 93, 32)
                imag = sampled(zero_taps, index + 1, weights, shift + 93, 32)
                turned = (real * cosine - imag * sine, real * sine + imag * cosine)
                for part in range(2):
                    if c == 0:
                        sums[q][part] = turned[part]
                    else:
                        sums[q][part] = sums[q][part] + turned[part]
        for q in range(2):
            for part in range(2):
                value = jnp.where(inside_one, sums[q][part], 0.0)
                index = (16 * q + i) * 2 + part
                one_taps[0, index] = value
                for t in range(1, 4):
                    one_taps[t, index] = shifted(value, t)
        return 0

    lax.fori_loop(0, 16, first_merge, 0)

    ramp_two = positions(8, 0).astype(jnp.float32) * (1.0 / bin_total) - 0.5

    def second_merge(i, _):
        p = block * 32 + i
        sums = [None, None]
        for c in range(2):
            beam = beam_two[c, p] - block * 16
            shift = shift_two[c, p]
            slope = 0.5 * (shift.astype(jnp.float32) + frac_two[c, p])
            cosine, sine = factors(base_two[c, p], slope, rows_out, ramp_two)
            weights = [
                taps[(c * (count_one + count_two) + count_one + p) * 8 + t] for t in range(8)
            ]
            index = (16 * c + beam) * 2
            real = sampled(one_taps, index, weights, shift + 29, rows_out)
            imag = sampled(one_taps, index + 1, weights, shift + 29, rows_out)
            turned = (real * cosine - imag * sine, real * sine + imag * cosine)
            for part in range(2):
                sums[part] = turned[part] if c == 0 else sums[part] + turned[part]
        for part in range(2):
            out_ref[2 * i + part] = sums[part].astype(out_ref.dtype)
        return 0

    lax.fori_loop(0, out_ref.shape[0] // 2, second_merge, 0)


def body(
    echo, chirp, beam_one, shift_one, frac_one, base_one, beam_two, shift_two, frac_two, base_two
):
    beams, _, bins = echo.shape[1:]
    chunks = bins // LANES
    taps = chirp.shape[1]
    arranged = echo[0].reshape(GROUP, 8, 2, chunks, LANES).transpose(0, 3, 2, 1, 4)
    arranged = arranged.reshape(GROUP, chunks, 16, LANES)
    vmem = pl.BlockSpec(memory_space=pltpu.VMEM)
    smem = pl.BlockSpec(memory_space=pltpu.SMEM)
    compressed = pl.pallas_call(
        gather_kernel,
        out_shape=jax.ShapeDtypeStruct((GROUP, 8 * 2 * 32, LANES), jnp.float32),
        in_specs=[vmem, pl.BlockSpec(memory_space=pl.ANY)],
        out_specs=vmem,
        scratch_shapes=[
            pltpu.VMEM((GROUP, LEFT + chunks + RIGHT, 16, LANES), jnp.bfloat16),
            pltpu.VMEM((512, 256 + taps), jnp.bfloat16),
            pltpu.SemaphoreType.DMA((3, GROUP)),
            pltpu.SemaphoreType.DMA((3, GROUP)),
            pltpu.SemaphoreType.DMA,
        ],
        compiler_params=pltpu.CompilerParams(
            collective_id=0, has_side_effects=True, vmem_limit_bytes=32 * 2**20
        ),
        name="gather_compress",
    )(chirp, arranged)

    fracs = jnp.concatenate([frac_one, frac_two], axis=1)
    spread = (jnp.arange(8).astype(jnp.float32) - 3.0)[None, None, :] - fracs[..., None]
    weights = jnp.sinc(spread) * (0.54 + 0.46 * jnp.cos(jnp.pi * spread / 4.0))
    merged = pl.pallas_call(
        merge_kernel,
        out_shape=jax.ShapeDtypeStruct((beams * 2, chunks, LANES), jnp.bfloat16),
        in_specs=[smem] * 9 + [vmem],
        out_specs=vmem,
        scratch_shapes=[
            pltpu.VMEM((4, GROUP * 8 * 2, 32, LANES), jnp.float32),
            pltpu.VMEM((4, 2 * 16 * 2, 32, LANES), jnp.float32),
        ],
        compiler_params=pltpu.CompilerParams(vmem_limit_bytes=32 * 2**20),
        name="merge",
    )(
        beam_one, shift_one, frac_one, base_one, beam_two, shift_two, frac_two, base_two,
        weights.reshape(-1), compressed.reshape(GROUP * 8 * 2, 32, LANES),
    )
    return merged.reshape(1, 1, beams, 2, bins)


def solution(mesh):
    in_specs = (
        P(("scene", "pulse"), "rep", None, "range"),
        P(),
        P(),
        P(),
        P(),
        P(),
        P(),
        P(),
        P(),
        P(),
    )
    out_specs = P("rep", ("scene", "pulse"), None, None, "range")
    return jax.shard_map(body, mesh=mesh, in_specs=in_specs, out_specs=out_specs, check_vma=False)
```

profile of v0, /device:TPU:11, one launch (start us, length us, event | category | flops | bytes accessed | tf_op | source)
XLA Modules:
  0.0 37.3 jit_solution(6941604334661092028)
XLA Ops:
  0.0 0.0 copy-start.1
  0.0 0.7 %copy-done.1 = f32[2,128]{1,0:T(2,128)S(1)} copy-done((f32[2,128]{1,0:T(2,128)S(1)}, f32[2,128]{1,0:T(2,128)}, u32[]{:S(2)}) %copy-start.1) | copy-done | bytes 1048
  0.7 0.7 %pad_maximum_fusion = f32[2,384]{1,0:T(2,128)S(1)} fusion(f32[2,256]{1,0:T(2,128)} %frac_two.1, f32[2,128]{1,0:T(2,128)S(1)} %copy-done.1), kind=kLoop, calls=%fused_computation.26 | loop fusion | flops 768 | bytes 6144 | tf_op jit(solution)/shard_map/concatenate | solution.py:336
  1.4 0.0 copy-start.9
  1.4 0.2 broadcast_subtract_fusion
  1.5 0.2 sub.34
  1.7 0.1 fusion.4.taps
  1.9 0.5 %copy-done.9 = bf16[1,32,2,3072]{3,2,1,0:T(2,128)(2,1)S(1)} copy-done((bf16[1,32,2,3072]{3,2,1,0:T(2,128)(2,1)S(1)}, bf16[1,32,2,3072]{3,2,1,0:T(2,128)(2,1)}, u32[]{:S(2)}) %copy-start.9) | copy-done | bytes 393240
  2.4 0.2 reshape_squeeze.3
  2.6 0.0 copy-start.2
  2.6 0.1 copy.14
  2.7 0.6 %copy-done.2 = bf16[2,512]{1,0:T(2,128)(2,1)S(1)} copy-done((bf16[2,512]{1,0:T(2,128)(2,1)S(1)}, bf16[2,512]{1,0:T(2,128)(2,1)}, u32[]{:S(2)}) %copy-start.2) | copy-done | bytes 2072
  3.3 0.0 copy-start
  3.3 0.0 copy-start.3
  3.3 0.0 copy-start.4
  3.3 0.0 copy-start.5
  3.3 0.0 copy-start.7
  3.3 0.0 copy-start.8
  3.3 15.7 %gather_compress.1 = f32[4,512,128]{2,1,0:T(8,128)S(1)} custom-call(bf16[2,512]{1,0:T(2,128)(2,1)S(1)} %copy-done.2, bf16[4,24,16,128]{3,2,1,0:T(8,128)(2,1)S(1)} %bitcast.7), custom_call_target="tpu_custom_call" | custom-call | tf_op jit(solution)/shard_map/gather_compress/pallas_call | solution.py:318
  19.1 0.0 copy-start.6
  19.1 0.0 copy-done
  19.1 0.0 copy-done.3
  19.1 0.0 copy-done.4
  19.1 0.0 copy-done.5
  19.1 0.0 copy-done.7
  19.1 0.0 copy-done.8
  19.1 0.6 %copy-done.6 = s32[2,128]{1,0:T(2,128)S(1)} copy-done((s32[2,128]{1,0:T(2,128)S(1)}, s32[2,128]{1,0:T(2,128)}, u32[]{:S(2)}) %copy-start.6) | copy-done | bytes 1048
  19.7 16.7 %merge.1 = bf16[64,24,128]{2,1,0:T(8,128)(2,1)S(1)} custom-call(s32[2,128]{1,0:T(2,128)S(1)} %copy-done.6, s32[2,128]{1,0:T(2,128)S(1)} %copy-done.7, f32[2,128]{1,0:T(2,128)S(1)} %copy-done.1, f32[2,128]{1,0:T(2,128)S(1)} %copy-done.8, s32[2,256]{1,0:T(2,128)S(1)} %copy-done.3, s32[2,256]{1,0:T(2,128)S(1)} %copy-done.4, f32[2,256]{1,0:T(2,128)S(1)} %copy-done, ...), custom_call_target="tpu_custom_call" | custom-call | tf_op jit(solution)/shard_map/merge/pallas_call | solution.py:339
  36.5 0.8 %reshape.21 = bf16[1,1,32,2,3072]{4,3,2,1,0:T(2,128)(2,1)} reshape(bf16[64,24,128]{2,1,0:T(8,128)(2,1)S(1)} %merge.1) | data formatting | bytes 786432 | tf_op jit(solution)/shard_map/reshape | solution.py:354
  (1 shorter events, 0.0 us)
Async XLA Ops:
  0.0 0.7 %copy-start.1 = (f32[2,128]{1,0:T(2,128)S(1)}, f32[2,128]{1,0:T(2,128)}, u32[]{:S(2)}) copy-start(f32[2,128]{1,0:T(2,128)} %frac_one.1) | copy-start | bytes 3076
  1.4 1.0 %copy-start.9 = (bf16[1,32,2,3072]{3,2,1,0:T(2,128)(2,1)S(1)}, bf16[1,32,2,3072]{3,2,1,0:T(2,128)(2,1)}, u32[]{:S(2)}) copy-start(bf16[1,32,2,3072]{3,2,1,0:T(2,128)(2,1)} %param.10) | copy-start | bytes 1179652
  2.6 0.7 %copy-start.2 = (bf16[2,512]{1,0:T(2,128)(2,1)S(1)}, bf16[2,512]{1,0:T(2,128)(2,1)}, u32[]{:S(2)}) copy-start(bf16[2,512]{1,0:T(2,128)(2,1)} %chirp_ref.1) | copy-start | bytes 6148
  3.3 15.8 %copy-start = (f32[2,256]{1,0:T(2,128)S(1)}, f32[2,256]{1,0:T(2,128)}, u32[]{:S(2)}) copy-start(f32[2,256]{1,0:T(2,128)} %frac_two.1) | copy-start | bytes 6148
  3.3 15.8 %copy-start.3 = (s32[2,256]{1,0:T(2,128)S(1)}, s32[2,256]{1,0:T(2,128)}, u32[]{:S(2)}) copy-start(s32[2,256]{1,0:T(2,128)} %beam_two.1) | copy-start | bytes 6148
  3.3 15.8 %copy-start.4 = (s32[2,256]{1,0:T(2,128)S(1)}, s32[2,256]{1,0:T(2,128)}, u32[]{:S(2)}) copy-start(s32[2,256]{1,0:T(2,128)} %shift_two.1) | copy-start | bytes 6148
  3.3 15.8 %copy-start.5 = (f32[2,256]{1,0:T(2,128)S(1)}, f32[2,256]{1,0:T(2,128)}, u32[]{:S(2)}) copy-start(f32[2,256]{1,0:T(2,128)} %base_two.1) | copy-start | bytes 6148
  3.3 15.8 %copy-start.7 = (s32[2,128]{1,0:T(2,128)S(1)}, s32[2,128]{1,0:T(2,128)}, u32[]{:S(2)}) copy-start(s32[2,128]{1,0:T(2,128)} %shift_one.1) | copy-start | bytes 3076
  3.3 15.8 %copy-start.8 = (f32[2,128]{1,0:T(2,128)S(1)}, f32[2,128]{1,0:T(2,128)}, u32[]{:S(2)}) copy-start(f32[2,128]{1,0:T(2,128)} %base_one.1) | copy-start | bytes 3076
  19.1 0.7 %copy-start.6 = (s32[2,128]{1,0:T(2,128)S(1)}, s32[2,128]{1,0:T(2,128)}, u32[]{:S(2)}) copy-start(s32[2,128]{1,0:T(2,128)} %beam_one.1) | copy-start | bytes 3076
where the time goes:
time: 37.5 us; the launch traced here: 37.3 us
  Pallas kernels  32.4 us (86%)
  local copies, waits for them, and re-layouts  3.77 us (10%)
  other arithmetic  0.98 us (3%)
    pallas_call x1, Pallas kernels, body(): pl.pallas_call(merge_kernel, out_shape=jax.ShapeDtypeStruct((beams * 2, c...  16.7 us
    pallas_call x1, Pallas kernels, body(): pl.pallas_call(gather_kernel, out_shape=jax.ShapeDtypeStruct((GROUP, 8 *...  15.7 us
    unnamed x20, local copies, waits for them, and re-layouts  2.37 us
    reshape x1, local copies, waits for them, and re-layouts, body(): return merged.reshape(1, 1, beams, 2, bins)  0.84 us

commit v1 on v0

v1 whole, which is shorter than its diff:
```python
import math

import jax
import jax.numpy as jnp
from jax import lax
from jax.experimental import pallas as pl
from jax.experimental.pallas import tpu as pltpu
from jax.sharding import PartitionSpec as P

LANES = 128
GROUP = 4
LEFT = 1
RIGHT = 5
ORDER = (1, 2, 3)
U_SPREAD, U_TURN, U_ONE, U_TWO = 8, 4, 4, 4
MESH = pl.DeviceIdType.MESH


def block_of(member):
    return 2 * lax.rem(member, 2) + member // 2


def shifted(value, distance):
    rows = value.shape[0]
    turned = pltpu.roll(value, LANES - distance, 1)
    below = pltpu.roll(turned, rows - 1, 0)
    lane = lax.broadcasted_iota(jnp.int32, value.shape, 1)
    return jnp.where(lane < LANES - distance, turned, below)


def cos_sin(angle):
    turns = angle * (1.0 / (2.0 * math.pi))
    turns = turns - jnp.round(turns)
    half = turns * math.pi
    square = half * half
    sine = jnp.full_like(half, -1.0 / math.factorial(11))
    for n in (9, 7, 5, 3, 1):
        sine = sine * square + (-1.0) ** ((n - 1) // 2) / math.factorial(n)
    sine = sine * half
    cosine = jnp.full_like(half, 1.0 / math.factorial(12))
    for n in (10, 8, 6, 4, 2, 0):
        cosine = cosine * square + (-1.0) ** (n // 2) / math.factorial(n)
    return 1.0 - 2.0 * sine * sine, 2.0 * sine * cosine


def partner(me, distance):
    member = me
    if distance % 2:
        member = member + 1 - 2 * lax.rem(me, 2)
    if distance // 2:
        member = member + 2 - 4 * (me // 2)
    return member


def kernel(
    chirp_ref, echo_ref, beam_one, shift_one, frac_one, base_one, beam_two, shift_two, frac_two,
    base_two, taps_ref, out_ref, ext, toeplitz, laid, zero_taps, one_taps, turn_one, turn_two, send_sem,
    recv_sem, local_sem,
):
    chunks = echo_ref.shape[1]
    taps = chirp_ref.shape[1]
    x = lax.axis_index("range")
    last = lax.axis_size("range") - 1
    z = lax.axis_index("pulse")
    first_member = z // GROUP * GROUP
    me = lax.rem(z, GROUP)
    has_left = x > 0
    has_right = x < last

    barrier = pltpu.get_barrier_semaphore()

    def greet(dx, dz):
        pl.semaphore_signal(
            barrier,
            inc=1,
            device_id={"range": x + dx, "pulse": first_member + partner(me, dz)},
            device_id_type=MESH,
        )

    for dz in range(1, GROUP):
        greet(0, dz)

    @pl.when(has_left)
    def _():
        for dz in range(GROUP):
            greet(-1, dz)

    @pl.when(has_right)
    def _():
        for dz in range(GROUP):
            greet(1, dz)

    def copy_to(kind, dz):
        member = partner(me, dz)
        block = block_of(member)
        dx = (0, -1, 1)[kind]
        start, count = ((0, chunks), (0, RIGHT), (chunks - LEFT, LEFT))[kind]
        target = (LEFT, LEFT + chunks, 0)[kind]
        return pltpu.make_async_remote_copy(
            src_ref=echo_ref.at[block, pl.ds(start, count)],
            dst_ref=ext.at[me, pl.ds(target, count)],
            send_sem=send_sem.at[kind, dz],
            recv_sem=recv_sem.at[kind, me],
            device_id={"range": x + dx, "pulse": first_member + member},
            device_id_type=MESH,
        )

    def arrival(kind, source):
        count = (chunks, RIGHT, LEFT)[kind]
        target = (LEFT, LEFT + chunks, 0)[kind]
        return pltpu.make_async_remote_copy(
            src_ref=ext.at[source, pl.ds(target, count)],
            dst_ref=ext.at[source, pl.ds(target, count)],
            send_sem=send_sem.at[kind, 0],
            recv_sem=recv_sem.at[kind, source],
            device_id={"range": x, "pulse": z},
            device_id_type=MESH,
        )

    own = pltpu.make_async_copy(
        echo_ref.at[block_of(me)], ext.at[me, pl.ds(LEFT, chunks)], local_sem
    )
    own.start()
    waits = GROUP - 1 + GROUP * (has_left.astype(jnp.int32) + has_right.astype(jnp.int32))
    pl.semaphore_wait(barrier, waits)

    def send_edges(dz):
        @pl.when(has_left)
        def _():
            copy_to(1, dz).start()

        @pl.when(has_right)
        def _():
            copy_to(2, dz).start()

    send_edges(0)
    for dz in ORDER:
        copy_to(0, dz).start()
        send_edges(dz)

    @pl.when(jnp.logical_not(has_right))
    def _():
        ext[:, LEFT + chunks :] = jnp.zeros((GROUP, RIGHT, 16, LANES), ext.dtype)

    @pl.when(jnp.logical_not(has_left))
    def _():
        ext[:, :LEFT] = jnp.zeros((GROUP, LEFT, 16, LANES), ext.dtype)

    span = 256 + taps
    for part in range(2):
        row = jnp.concatenate(
            [chirp_ref[part : part + 1, :].astype(jnp.float32), jnp.zeros((1, 256), jnp.float32)],
            axis=1,
        )
        rows = jnp.broadcast_to(row, (256, span))
        rolled = pltpu.roll(rows, 0, 1, stride=1, stride_axis=0)
        toeplitz[256 * part : 256 * (part + 1), :] = rolled.astype(toeplitz.dtype)

    out_blocks = (chunks + 2) // 2
    left_scale = has_left.astype(jnp.float32)
    right_scale = has_right.astype(jnp.float32)

    count_one = beam_one.shape[1]
    count_two = beam_two.shape[1]
    rows_out = out_ref.shape[1]
    bins = rows_out * LANES
    bin_total = bins * lax.axis_size("range")
    first_bin = x * bins
    block = 4 * lax.axis_index("rep") + block_of(me)

    def positions(rows, margin):
        row = lax.broadcasted_iota(jnp.int32, (rows, LANES), 0)
        lane = lax.broadcasted_iota(jnp.int32, (rows, LANES), 1)
        return first_bin - margin + row * LANES + lane

    def factors(base, slope, rows, ramp):
        cosine, sine = cos_sin(base + slope * ramp)
        step = jnp.full((8, LANES), slope * (8.0 * LANES / bin_total), jnp.float32)
        step_cos, step_sin = cos_sin(step)
        cosines, sines = [cosine], [sine]
        for _ in range(rows // 8 - 1):
            cosine, sine = cosine * step_cos - sine * step_sin, sine * step_cos + cosine * step_sin
            cosines.append(cosine)
            sines.append(sine)
        return jnp.concatenate(cosines, 0), jnp.concatenate(sines, 0)

    def sampled(load, weights, distance, rows):
        value = load(0)
        early = weights[0] * value
        late = weights[4] * value
        for t in range(1, 4):
            value = load(t)
            early = early + weights[t] * value
            late = late + weights[t + 4] * value
        return shifted(early + shifted(late, 4), distance)[:rows]

    ramp_one = positions(8, 32).astype(jnp.float32) * (1.0 / bin_total) - 0.5
    place_one = positions(32, 32)
    inside_one = (place_one >= 0) & (place_one < bin_total)

    ramp_two = positions(8, 0).astype(jnp.float32) * (1.0 / bin_total) - 0.5

    def turns(i, _):
        for c in range(2):
            p = block * 32 + i
            slope = 0.5 * (shift_two[c, p].astype(jnp.float32) + frac_two[c, p])
            cosine, sine = factors(base_two[c, p], slope, rows_out, ramp_two)
            turn_two[(2 * i + c) * 2] = cosine
            turn_two[(2 * i + c) * 2 + 1] = sine
        return 0

    def turns_one(i, _):
        for c in range(2):
            p = block * 16 + i
            slope = 0.5 * (shift_one[c, p].astype(jnp.float32) + frac_one[c, p])
            cosine, sine = factors(base_one[c, p], slope, 32, ramp_one)
            turn_one[(2 * i + c) * 2] = cosine
            turn_one[(2 * i + c) * 2 + 1] = sine
        return 0

    lax.fori_loop(0, 16, turns_one, 0, unroll=U_TURN)
    lax.fori_loop(0, 32, turns, 0, unroll=U_TURN)

    def compress(dz):
        source = partner(me, dz)
        if dz == 0:
            own.wait()
        else:
            arrival(0, source).wait_recv()

        @pl.when(has_right)
        def _():
            arrival(1, source).wait_recv()

        @pl.when(has_left)
        def _():
            arrival(2, source).wait_recv()

        held = ext[source].reshape((LEFT + chunks + RIGHT) // 2, 2, 16, LANES)
        pieces = [
            held[u // 2 : u // 2 + out_blocks, u % 2].reshape(out_blocks * 16, LANES)
            for u in range(span // LANES)
        ]
        windows = jnp.concatenate(pieces, axis=1)
        product = lax.dot_general(
            windows, toeplitz[...], (((1,), (1,)), ((), ())), preferred_element_type=jnp.float32
        )
        for block in range(out_blocks):
            up = product[16 * block : 16 * block + 8]
            down = product[16 * block + 8 : 16 * block + 16]
            values = (up[:, :256] + down[:, 256:], down[:, :256] - up[:, 256:])
            for half in range(2):
                chunk = 2 * block + half
                for part in range(2):
                    value = values[part][:, half * LANES : (half + 1) * LANES]
                    if chunk == 0:
                        value = value * left_scale
                    if chunk == chunks + 1:
                        value = value * right_scale
                    laid[pl.ds(32 * part + chunk, 8, stride=64), :] = value

        def spread(index, _):
            rows = pl.ds(pl.multiple_of(index * 32, 32), 32)
            value = laid[rows]
            zero_taps[0, source * 16 + index] = value
            for t in range(1, 4):
                zero_taps[t, source * 16 + index] = shifted(value, t)
            return 0

        lax.fori_loop(0, 16, spread, 0, unroll=U_SPREAD)

    def first_merges(q):
        def first_merge(i, _):
            p = block * 16 + i
            sums = [None, None]
            for c in range(2):
                beam = jnp.clip(beam_one[c, p] - block * 8, 0, 7)
                distance = shift_one[c, p] + 93
                weights = [taps_ref[(c * (count_one + count_two) + p) * 8 + t] for t in range(8)]
                parts = []
                for part in range(2):
                    index = (2 * q + c) * 16 + beam * 2 + part
                    parts.append(sampled(lambda t: zero_taps[t, index], weights, distance, 32))
                real, imag = parts
                cosine = turn_one[(2 * i + c) * 2]
                sine = turn_one[(2 * i + c) * 2 + 1]
                turned = (real * cosine - imag * sine, real * sine + imag * cosine)
                for part in range(2):
                    sums[part] = turned[part] if c == 0 else sums[part] + turned[part]
            for part in range(2):
                value = jnp.where(inside_one, sums[part], 0.0)
                index = (16 * q + i) * 2 + part
                one_taps[0, index] = value
                for t in range(1, 4):
                    one_taps[t, index] = shifted(value, t)
            return 0

        lax.fori_loop(0, 16, first_merge, 0, unroll=U_ONE)

    def second_merge(i, _):
        p = block * 32 + i
        sums = [None, None]
        for c in range(2):
            beam = jnp.clip(beam_two[c, p] - block * 16, 0, 15)
            distance = shift_two[c, p] + 29
            weights = [
                taps_ref[(c * (count_one + count_two) + count_one + p) * 8 + t] for t in range(8)
            ]
            parts = []
            for part in range(2):
                index = (16 * c + beam) * 2 + part
                parts.append(sampled(lambda t: one_taps[t, index], weights, distance, rows_out))
            real, imag = parts
            cosine = turn_two[(2 * i + c) * 2]
            sine = turn_two[(2 * i + c) * 2 + 1]
            turned = (real * cosine - imag * sine, real * sine + imag * cosine)
            for part in range(2):
                sums[part] = turned[part] if c == 0 else sums[part] + turned[part]
        for part in range(2):
            out_ref[2 * i + part] = sums[part].astype(out_ref.dtype)
        return 0

    compress(0)
    compress(1)
    first_merges(me // 2)
    compress(2)
    compress(3)
    first_merges(1 - me // 2)
    lax.fori_loop(0, 32, second_merge, 0, unroll=U_TWO)

    for dz in range(GROUP):

        @pl.when(has_left)
        def _():
            copy_to(1, dz).wait_send()

        @pl.when(has_right)
        def _():
            copy_to(2, dz).wait_send()

        if dz:
            copy_to(0, dz).wait_send()


def body(
    echo, chirp, beam_one, shift_one, frac_one, base_one, beam_two, shift_two, frac_two, base_two
):
    beams, _, bins = echo.shape[1:]
    chunks = bins // LANES
    taps = chirp.shape[1]
    arranged = echo[0].reshape(GROUP, 8, 2, chunks, LANES).transpose(0, 3, 2, 1, 4)
    arranged = arranged.reshape(GROUP, chunks, 16, LANES)
    vmem = pl.BlockSpec(memory_space=pltpu.VMEM)
    smem = pl.BlockSpec(memory_space=pltpu.SMEM)
    fracs = jnp.concatenate([frac_one, frac_two], axis=1)
    spread = (jnp.arange(8).astype(jnp.float32) - 3.0)[None, None, :] - fracs[..., None]
    weights = jnp.sinc(spread) * (0.54 + 0.46 * jnp.cos(jnp.pi * spread / 4.0))
    merged = pl.pallas_call(
        kernel,
        out_shape=jax.ShapeDtypeStruct((beams * 2, chunks, LANES), jnp.bfloat16),
        in_specs=[vmem, pl.BlockSpec(memory_space=pl.ANY)] + [smem] * 9,
        out_specs=vmem,
        scratch_shapes=[
            pltpu.VMEM((GROUP, LEFT + chunks + RIGHT, 16, LANES), jnp.bfloat16),
            pltpu.VMEM((512, 256 + taps), jnp.bfloat16),
            pltpu.VMEM((8 * 2 * 32, LANES), jnp.float32),
            pltpu.VMEM((4, GROUP * 16, 32, LANES), jnp.float32),
            pltpu.VMEM((4, 2 * 16 * 2, 32, LANES), jnp.float32),
            pltpu.VMEM((16 * 2 * 2, 32, LANES), jnp.float32),
            pltpu.VMEM((32 * 2 * 2, chunks, LANES), jnp.float32),
            pltpu.SemaphoreType.DMA((3, GROUP)),
            pltpu.SemaphoreType.DMA((3, GROUP)),
            pltpu.SemaphoreType.DMA,
        ],
        compiler_params=pltpu.CompilerParams(
            collective_id=0, has_side_effects=True, vmem_limit_bytes=40 * 2**20
        ),
        name="merge_all",
    )(
        chirp, arranged, beam_one, shift_one, frac_one, base_one, beam_two, shift_two, frac_two,
        base_two, weights.reshape(-1),
    )
    return merged.reshape(1, 1, beams, 2, bins)


def solution(mesh):
    in_specs = (
        P(("scene", "pulse"), "rep", None, "range"),
        P(),
        P(),
        P(),
        P(),
        P(),
        P(),
        P(),
        P(),
        P(),
    )
    out_specs = P("rep", ("scene", "pulse"), None, None, "range")
    return jax.shard_map(body, mesh=mesh, in_specs=in_specs, out_specs=out_specs, check_vma=False)
```

time: 37.5 us -> 27.5 us (0.73)
  the two profiles are of different devices: /device:TPU:11 before, /device:TPU:0 now
where the time goes in v1:
time: 27.5 us; the launch traced here: 27.2 us
  Pallas kernels  22.9 us (83%)
  local copies, waits for them, and re-layouts  3.26 us (12%)
  other arithmetic  0.98 us (4%)
    pallas_call x1, Pallas kernels, body(): pl.pallas_call(kernel, out_shape=jax.ShapeDtypeStruct((beams * 2, chunks,...  22.9 us
    unnamed x20, local copies, waits for them, and re-layouts  1.87 us
    reshape x1, local copies, waits for them, and re-layouts, body(): return merged.reshape(1, 1, beams, 2, bins)  0.84 us
    concatenate x1, other arithmetic, body(): fracs = jnp.concatenate([frac_one, frac_two], axis=1)  0.69 us

profile of v1, /device:TPU:0, one launch (start us, length us, event | category | flops | bytes accessed | tf_op | source)
XLA Modules:
  0.0 27.2 jit_solution(3692968637320982909)
XLA Ops:
  0.0 0.0 copy-start.1
  0.0 0.7 %copy-done.1 = f32[2,128]{1,0:T(2,128)S(1)} copy-done((f32[2,128]{1,0:T(2,128)S(1)}, f32[2,128]{1,0:T(2,128)}, u32[]{:S(2)}) %copy-start.1) | copy-done | bytes 1048
  0.7 0.7 %pad_maximum_fusion = f32[2,384]{1,0:T(2,128)S(1)} fusion(f32[2,256]{1,0:T(2,128)} %frac_two.1, f32[2,128]{1,0:T(2,128)S(1)} %copy-done.1), kind=kLoop, calls=%fused_computation.26 | loop fusion | flops 768 | bytes 6144 | tf_op jit(solution)/shard_map/concatenate | solution.py:355
  1.4 0.0 copy-start.9
  1.4 0.2 broadcast_subtract_fusion
  1.5 0.2 sub.34
  1.7 0.1 fusion.4.taps_ref
  1.9 0.5 %copy-done.9 = bf16[1,32,2,3072]{3,2,1,0:T(2,128)(2,1)S(1)} copy-done((bf16[1,32,2,3072]{3,2,1,0:T(2,128)(2,1)S(1)}, bf16[1,32,2,3072]{3,2,1,0:T(2,128)(2,1)}, u32[]{:S(2)}) %copy-start.9) | copy-done | bytes 393240
  2.4 0.2 reshape_squeeze.3
  2.6 0.0 copy-start
  2.6 0.0 copy-start.2
  2.6 0.0 copy-start.3
  2.7 0.0 copy-start.4
  2.7 0.0 copy-start.5
  2.7 0.0 copy-start.7
  2.7 0.0 copy-start.8
  2.7 0.1 copy.14
  2.8 0.0 copy-start.6
  2.8 0.5 %copy-done = f32[2,256]{1,0:T(2,128)S(1)} copy-done((f32[2,256]{1,0:T(2,128)S(1)}, f32[2,256]{1,0:T(2,128)}, u32[]{:S(2)}) %copy-start) | copy-done | bytes 2072
  3.3 0.0 copy-done.2
  3.3 0.0 copy-done.3
  3.3 0.0 copy-done.4
  3.3 0.0 copy-done.5
  3.4 0.0 copy-done.7
  3.4 0.0 copy-done.8
  3.4 0.1 copy-done.6
  3.5 22.9 %merge_all.1 = bf16[64,24,128]{2,1,0:T(8,128)(2,1)S(1)} custom-call(bf16[2,512]{1,0:T(2,128)(2,1)S(1)} %copy-done.2, bf16[4,24,16,128]{3,2,1,0:T(8,128)(2,1)S(1)} %bitcast.5, s32[2,128]{1,0:T(2,128)S(1)} %copy-done.6, s32[2,128]{1,0:T(2,128)S(1)} %copy-done.7, f32[2,128]{1,0:T(2,128)S(1)} %copy-done.1, f32[2,128]{1,0:T(2,128)S(1)} %copy-done.8, ...), custom_call_target="tpu_custom_call" | custom-call | tf_op jit(solution)/shard_map/merge_all/pallas_call | solution.py:358
  26.4 0.8 %reshape.17 = bf16[1,1,32,2,3072]{4,3,2,1,0:T(2,128)(2,1)} reshape(bf16[64,24,128]{2,1,0:T(8,128)(2,1)S(1)} %merge_all.1) | data formatting | bytes 786432 | tf_op jit(solution)/shard_map/reshape | solution.py:383
  (1 shorter events, 0.0 us)
Async XLA Ops:
  0.0 0.7 %copy-start.1 = (f32[2,128]{1,0:T(2,128)S(1)}, f32[2,128]{1,0:T(2,128)}, u32[]{:S(2)}) copy-start(f32[2,128]{1,0:T(2,128)} %frac_one.1) | copy-start | bytes 3076
  1.4 1.0 %copy-start.9 = (bf16[1,32,2,3072]{3,2,1,0:T(2,128)(2,1)S(1)}, bf16[1,32,2,3072]{3,2,1,0:T(2,128)(2,1)}, u32[]{:S(2)}) copy-start(bf16[1,32,2,3072]{3,2,1,0:T(2,128)(2,1)} %param.10) | copy-start | bytes 1179652
  2.6 0.7 %copy-start = (f32[2,256]{1,0:T(2,128)S(1)}, f32[2,256]{1,0:T(2,128)}, u32[]{:S(2)}) copy-start(f32[2,256]{1,0:T(2,128)} %frac_two.1) | copy-start | bytes 6148
  2.6 0.7 %copy-start.2 = (bf16[2,512]{1,0:T(2,128)(2,1)S(1)}, bf16[2,512]{1,0:T(2,128)(2,1)}, u32[]{:S(2)}) copy-start(bf16[2,512]{1,0:T(2,128)(2,1)} %chirp_ref.1) | copy-start | bytes 6148
  2.6 0.7 %copy-start.3 = (s32[2,256]{1,0:T(2,128)S(1)}, s32[2,256]{1,0:T(2,128)}, u32[]{:S(2)}) copy-start(s32[2,256]{1,0:T(2,128)} %beam_two.1) | copy-start | bytes 6148
  2.7 0.7 %copy-start.4 = (s32[2,256]{1,0:T(2,128)S(1)}, s32[2,256]{1,0:T(2,128)}, u32[]{:S(2)}) copy-start(s32[2,256]{1,0:T(2,128)} %shift_two.1) | copy-start | bytes 6148
  2.7 0.7 %copy-start.5 = (f32[2,256]{1,0:T(2,128)S(1)}, f32[2,256]{1,0:T(2,128)}, u32[]{:S(2)}) copy-start(f32[2,256]{1,0:T(2,128)} %base_two.1) | copy-start | bytes 6148
  2.7 0.7 %copy-start.7 = (s32[2,128]{1,0:T(2,128)S(1)}, s32[2,128]{1,0:T(2,128)}, u32[]{:S(2)}) copy-start(s32[2,128]{1,0:T(2,128)} %shift_one.1) | copy-start | bytes 3076
  2.7 0.7 %copy-start.8 = (f32[2,128]{1,0:T(2,128)S(1)}, f32[2,128]{1,0:T(2,128)}, u32[]{:S(2)}) copy-start(f32[2,128]{1,0:T(2,128)} %base_one.1) | copy-start | bytes 3076
  2.8 0.7 %copy-start.6 = (s32[2,128]{1,0:T(2,128)S(1)}, s32[2,128]{1,0:T(2,128)}, u32[]{:S(2)}) copy-start(s32[2,128]{1,0:T(2,128)} %beam_one.1) | copy-start | bytes 3076

commit v2 on v1

--- a/solution.py
+++ b/solution.py
@@ -43,6 +43,20 @@
     return 1.0 - 2.0 * sine * sine, 2.0 * sine * cosine
 
 
+def tap_weights(frac):
+    tap = lax.broadcasted_iota(jnp.int32, frac.shape, 0)
+    spread = (tap.astype(jnp.float32) - 3.0) - frac
+    near = jnp.minimum(frac, 1.0 - frac) * math.pi
+    square = near * near
+    sine = jnp.full_like(near, -1.0 / math.factorial(11))
+    for n in (9, 7, 5, 3, 1):
+        sine = sine * square + (-1.0) ** ((n - 1) // 2) / math.factorial(n)
+    sine = jnp.where(lax.rem(tap, 2) == 0, sine, -sine) * near
+    exact = spread == 0.0
+    sinc = jnp.where(exact, 1.0, sine / jnp.where(exact, 1.0, math.pi * spread))
+    return sinc * (0.54 + 0.46 * cos_sin(spread * (math.pi / 4.0))[0])
+
+
 def partner(me, distance):
     member = me
     if distance % 2:
@@ -54,8 +68,8 @@
 
 def kernel(
     chirp_ref, echo_ref, beam_one, shift_one, frac_one, base_one, beam_two, shift_two, frac_two,
-    base_two, taps_ref, out_ref, ext, toeplitz, laid, zero_taps, one_taps, turn_one, turn_two, send_sem,
-    recv_sem, local_sem,
+    base_two, fracs_one, fracs_two, out_ref, ext, taps_held, taps_ref, toeplitz, laid, zero_taps, one_taps, turn_one, turn_two, send_sem,
+    recv_sem, local_sem, taps_sem,
 ):
     chunks = echo_ref.shape[1]
     taps = chirp_ref.shape[1]
@@ -161,12 +175,18 @@
     right_scale = has_right.astype(jnp.float32)
 
     count_one = beam_one.shape[1]
-    count_two = beam_two.shape[1]
     rows_out = out_ref.shape[1]
     bins = rows_out * LANES
     bin_total = bins * lax.axis_size("range")
     first_bin = x * bins
     block = 4 * lax.axis_index("rep") + block_of(me)
+
+    for c in range(2):
+        frac = jnp.concatenate([fracs_one[c : c + 1, :], fracs_two[c : c + 1, :]], axis=1)
+        frac = jnp.broadcast_to(frac, (8, frac.shape[1]))
+        taps_held[8 * c : 8 * (c + 1), :] = tap_weights(frac)
+    taps_copy = pltpu.make_async_copy(taps_held, taps_ref, taps_sem)
+    taps_copy.start()
 
     def positions(rows, margin):
         row = lax.broadcasted_iota(jnp.int32, (rows, LANES), 0)
@@ -276,7 +296,7 @@
             for c in range(2):
                 beam = jnp.clip(beam_one[c, p] - block * 8, 0, 7)
                 distance = shift_one[c, p] + 93
-                weights = [taps_ref[(c * (count_one + count_two) + p) * 8 + t] for t in range(8)]
+                weights = [taps_ref[8 * c + t, p] for t in range(8)]
                 parts = []
                 for part in range(2):
                     index = (2 * q + c) * 16 + beam * 2 + part
@@ -304,7 +324,7 @@
             beam = jnp.clip(beam_two[c, p] - block * 16, 0, 15)
             distance = shift_two[c, p] + 29
             weights = [
-                taps_ref[(c * (count_one + count_two) + count_one + p) * 8 + t] for t in range(8)
+                taps_ref[8 * c + t, count_one + p] for t in range(8)
             ]
             parts = []
             for part in range(2):
@@ -320,6 +340,7 @@
             out_ref[2 * i + part] = sums[part].astype(out_ref.dtype)
         return 0
 
+    taps_copy.wait()
     compress(0)
     compress(1)
     first_merges(me // 2)
@@ -348,20 +369,20 @@
     beams, _, bins = echo.shape[1:]
     chunks = bins // LANES
     taps = chirp.shape[1]
+    fracs = frac_one.shape[1] + frac_two.shape[1]
     arranged = echo[0].reshape(GROUP, 8, 2, chunks, LANES).transpose(0, 3, 2, 1, 4)
     arranged = arranged.reshape(GROUP, chunks, 16, LANES)
     vmem = pl.BlockSpec(memory_space=pltpu.VMEM)
     smem = pl.BlockSpec(memory_space=pltpu.SMEM)
-    fracs = jnp.concatenate([frac_one, frac_two], axis=1)
-    spread = (jnp.arange(8).astype(jnp.float32) - 3.0)[None, None, :] - fracs[..., None]
-    weights = jnp.sinc(spread) * (0.54 + 0.46 * jnp.cos(jnp.pi * spread / 4.0))
     merged = pl.pallas_call(
         kernel,
         out_shape=jax.ShapeDtypeStruct((beams * 2, chunks, LANES), jnp.bfloat16),
-        in_specs=[vmem, pl.BlockSpec(memory_space=pl.ANY)] + [smem] * 9,
+        in_specs=[vmem, pl.BlockSpec(memory_space=pl.ANY)] + [smem] * 8 + [vmem] * 2,
         out_specs=vmem,
         scratch_shapes=[
             pltpu.VMEM((GROUP, LEFT + chunks + RIGHT, 16, LANES), jnp.bfloat16),
+            pltpu.VMEM((16, fracs), jnp.float32),
+            pltpu.SMEM((16, fracs), jnp.float32),
             pltpu.VMEM((512, 256 + taps), jnp.bfloat16),
             pltpu.VMEM((8 * 2 * 32, LANES), jnp.float32),
             pltpu.VMEM((4, GROUP * 16, 32, LANES), jnp.float32),
@@ -371,6 +392,7 @@
             pltpu.SemaphoreType.DMA((3, GROUP)),
             pltpu.SemaphoreType.DMA((3, GROUP)),
             pltpu.SemaphoreType.DMA,
+            pltpu.SemaphoreType.DMA,
         ],
         compiler_params=pltpu.CompilerParams(
             collective_id=0, has_side_effects=True, vmem_limit_bytes=40 * 2**20
@@ -378,7 +400,7 @@
         name="merge_all",
     )(
         chirp, arranged, beam_one, shift_one, frac_one, base_one, beam_two, shift_two, frac_two,
-        base_two, weights.reshape(-1),
+        base_two, frac_one, frac_two,
     )
     return merged.reshape(1, 1, beams, 2, bins)
 

time: 27.5 us -> 25.8 us (0.938)
  other arithmetic: 0.98 us -> 0 us
  local copies, waits for them, and re-layouts: 3.26 us -> 2.89 us
  Pallas kernels: 22.9 us -> 22.6 us
    unnamed x20 -> x18, local copies, waits for them, and re-layouts: 1.87 us -> 0.7 us
    another operation x2, local copies, waits for them, and re-layouts: 0.35 us -> 1.35 us  [body(): echo[0].reshape(GROUP, 8, 2, chunks, LANES).transpose(0, 3, 2, 1, 4)]
    concatenate x1 -> x0, other arithmetic: 0.69 us -> none  [body(): fracs = jnp.concatenate([frac_one, frac_two], axis=1)]
where the time goes in v2:
time: 25.8 us; the launch traced here: 25.6 us
  Pallas kernels  22.6 us (88%)
  local copies, waits for them, and re-layouts  2.89 us (11%)
    pallas_call x1, Pallas kernels, body(): pl.pallas_call(kernel, out_shape=jax.ShapeDtypeStruct((beams * 2, chunks,...  22.6 us
    another operation x2, local copies, waits for them, and re-layouts, body(): echo[0].reshape(GROUP, 8, 2, chunks, LANES).transpose(0, 3, 2, 1, 4)  1.35 us
    reshape x1, local copies, waits for them, and re-layouts, body(): return merged.reshape(1, 1, beams, 2, bins)  0.84 us
    unnamed x18, local copies, waits for them, and re-layouts  0.7 us

profile of v2, /device:TPU:0, one launch (start us, length us, event | category | flops | bytes accessed | tf_op | source)
XLA Modules:
  0.0 25.6 jit_solution(11115153967368156670)
XLA Ops:
  0.0 1.2 %reshape_squeeze.3 = bf16[4,8,2,24,128]{4,3,2,1,0:T(8,128)(2,1)S(1)} reshape(bf16[1,32,2,3072]{3,2,1,0:T(2,128)(2,1)} %param.10) | data formatting | bytes 786432 | tf_op jit(solution)/shard_map/reshape;squeeze | solution.py:373
  1.2 0.0 copy-start
  1.3 0.0 copy-start.2
  1.3 0.0 copy-start.3
  1.3 0.0 copy-start.4
  1.3 0.0 copy-start.5
  1.3 0.0 copy-start.6
  1.3 0.0 copy-start.7
  1.3 0.0 copy-start.8
  1.3 0.1 copy.13
  1.5 0.0 copy-start.1
  1.5 0.5 %copy-done = f32[2,256]{1,0:T(2,128)S(1)} copy-done((f32[2,256]{1,0:T(2,128)S(1)}, f32[2,256]{1,0:T(2,128)}, u32[]{:S(2)}) %copy-start) | copy-done | bytes 2072
  1.9 0.0 copy-done.2
  1.9 0.0 copy-done.3
  2.0 0.0 copy-done.4
  2.0 0.0 copy-done.5
  2.0 0.0 copy-done.6
  2.0 0.0 copy-done.7
  2.0 0.0 copy-done.8
  2.0 0.1 copy-done.1
  2.1 22.6 %merge_all.1 = bf16[64,24,128]{2,1,0:T(8,128)(2,1)S(1)} custom-call(bf16[2,512]{1,0:T(2,128)(2,1)S(1)} %copy-done.2, bf16[4,24,16,128]{3,2,1,0:T(8,128)(2,1)S(1)} %bitcast.5, s32[2,128]{1,0:T(2,128)S(1)} %copy-done.6, s32[2,128]{1,0:T(2,128)S(1)} %copy-done.7, f32[2,128]{1,0:T(2,128)S(1)} %copy-done.1, f32[2,128]{1,0:T(2,128)S(1)} %copy-done.8, ...), custom_call_target="tpu_custom_call" | custom-call | tf_op jit(solution)/shard_map/merge_all/pallas_call | solution.py:377
  24.8 0.8 %reshape.7 = bf16[1,1,32,2,3072]{4,3,2,1,0:T(2,128)(2,1)} reshape(bf16[64,24,128]{2,1,0:T(8,128)(2,1)S(1)} %merge_all.1) | data formatting | bytes 786432 | tf_op jit(solution)/shard_map/reshape | solution.py:405
Async XLA Ops:
  1.2 0.7 %copy-start = (f32[2,256]{1,0:T(2,128)S(1)}, f32[2,256]{1,0:T(2,128)}, u32[]{:S(2)}) copy-start(f32[2,256]{1,0:T(2,128)} %fracs_two.1) | copy-start | bytes 6148
  1.3 0.7 %copy-start.2 = (bf16[2,512]{1,0:T(2,128)(2,1)S(1)}, bf16[2,512]{1,0:T(2,128)(2,1)}, u32[]{:S(2)}) copy-start(bf16[2,512]{1,0:T(2,128)(2,1)} %chirp_ref.1) | copy-start | bytes 6148
  1.3 0.7 %copy-start.3 = (s32[2,256]{1,0:T(2,128)S(1)}, s32[2,256]{1,0:T(2,128)}, u32[]{:S(2)}) copy-start(s32[2,256]{1,0:T(2,128)} %beam_two.1) | copy-start | bytes 6148
  1.3 0.7 %copy-start.4 = (s32[2,256]{1,0:T(2,128)S(1)}, s32[2,256]{1,0:T(2,128)}, u32[]{:S(2)}) copy-start(s32[2,256]{1,0:T(2,128)} %shift_two.1) | copy-start | bytes 6148
  1.3 0.7 %copy-start.5 = (f32[2,256]{1,0:T(2,128)S(1)}, f32[2,256]{1,0:T(2,128)}, u32[]{:S(2)}) copy-start(f32[2,256]{1,0:T(2,128)} %base_two.1) | copy-start | bytes 6148
  1.3 0.7 %copy-start.6 = (s32[2,128]{1,0:T(2,128)S(1)}, s32[2,128]{1,0:T(2,128)}, u32[]{:S(2)}) copy-start(s32[2,128]{1,0:T(2,128)} %beam_one.1) | copy-start | bytes 3076
  1.3 0.7 %copy-start.7 = (s32[2,128]{1,0:T(2,128)S(1)}, s32[2,128]{1,0:T(2,128)}, u32[]{:S(2)}) copy-start(s32[2,128]{1,0:T(2,128)} %shift_one.1) | copy-start | bytes 3076
  1.3 0.7 %copy-start.8 = (f32[2,128]{1,0:T(2,128)S(1)}, f32[2,128]{1,0:T(2,128)}, u32[]{:S(2)}) copy-start(f32[2,128]{1,0:T(2,128)} %base_one.1) | copy-start | bytes 3076
  1.5 0.7 %copy-start.1 = (f32[2,128]{1,0:T(2,128)S(1)}, f32[2,128]{1,0:T(2,128)}, u32[]{:S(2)}) copy-start(f32[2,128]{1,0:T(2,128)} %fracs_one.1) | copy-start | bytes 3076

commit v3 on v2

--- a/solution.py
+++ b/solution.py
@@ -12,7 +12,7 @@
 LEFT = 1
 RIGHT = 5
 ORDER = (1, 2, 3)
-U_SPREAD, U_TURN, U_ONE, U_TWO = 8, 4, 4, 4
+U_SPREAD, U_TURN, U_ONE, U_TWO = 16, 4, 4, 4
 MESH = pl.DeviceIdType.MESH
 
 

time: 25.8 us -> 25.6 us (level)
  no operation moved by 1% of the time
where the time goes in v3:
time: 25.6 us; the launch traced here: 25.4 us
  Pallas kernels  22.4 us (88%)
  local copies, waits for them, and re-layouts  2.89 us (11%)
    pallas_call x1, Pallas kernels, body(): pl.pallas_call(kernel, out_shape=jax.ShapeDtypeStruct((beams * 2, chunks,...  22.4 us
    another operation x2, local copies, waits for them, and re-layouts, body(): echo[0].reshape(GROUP, 8, 2, chunks, LANES).transpose(0, 3, 2, 1, 4)  1.35 us
    reshape x1, local copies, waits for them, and re-layouts, body(): return merged.reshape(1, 1, beams, 2, bins)  0.84 us
    unnamed x18, local copies, waits for them, and re-layouts  0.7 us

profile of v3, /device:TPU:0, one launch (start us, length us, event | category | flops | bytes accessed | tf_op | source)
XLA Modules:
  0.0 25.4 jit_solution(8751878629232097521)
XLA Ops:
  0.0 1.2 %reshape_squeeze.3 = bf16[4,8,2,24,128]{4,3,2,1,0:T(8,128)(2,1)S(1)} reshape(bf16[1,32,2,3072]{3,2,1,0:T(2,128)(2,1)} %param.10) | data formatting | bytes 786432 | tf_op jit(solution)/shard_map/reshape;squeeze | solution.py:373
  1.2 0.0 copy-start
  1.3 0.0 copy-start.2
  1.3 0.0 copy-start.3
  1.3 0.0 copy-start.4
  1.3 0.0 copy-start.5
  1.3 0.0 copy-start.6
  1.3 0.0 copy-start.7
  1.3 0.0 copy-start.8
  1.3 0.1 copy.13
  1.5 0.0 copy-start.1
  1.5 0.5 %copy-done = f32[2,256]{1,0:T(2,128)S(1)} copy-done((f32[2,256]{1,0:T(2,128)S(1)}, f32[2,256]{1,0:T(2,128)}, u32[]{:S(2)}) %copy-start) | copy-done | bytes 2072
  1.9 0.0 copy-done.2
  1.9 0.0 copy-done.3
  2.0 0.0 copy-done.4
  2.0 0.0 copy-done.5
  2.0 0.0 copy-done.6
  2.0 0.0 copy-done.7
  2.0 0.0 copy-done.8
  2.0 0.1 copy-done.1
  2.1 22.4 %merge_all.1 = bf16[64,24,128]{2,1,0:T(8,128)(2,1)S(1)} custom-call(bf16[2,512]{1,0:T(2,128)(2,1)S(1)} %copy-done.2, bf16[4,24,16,128]{3,2,1,0:T(8,128)(2,1)S(1)} %bitcast.5, s32[2,128]{1,0:T(2,128)S(1)} %copy-done.6, s32[2,128]{1,0:T(2,128)S(1)} %copy-done.7, f32[2,128]{1,0:T(2,128)S(1)} %copy-done.1, f32[2,128]{1,0:T(2,128)S(1)} %copy-done.8, ...), custom_call_target="tpu_custom_call" | custom-call | tf_op jit(solution)/shard_map/merge_all/pallas_call | solution.py:377
  24.5 0.8 %reshape.7 = bf16[1,1,32,2,3072]{4,3,2,1,0:T(2,128)(2,1)} reshape(bf16[64,24,128]{2,1,0:T(8,128)(2,1)S(1)} %merge_all.1) | data formatting | bytes 786432 | tf_op jit(solution)/shard_map/reshape | solution.py:405
Async XLA Ops:
  1.2 0.7 %copy-start = (f32[2,256]{1,0:T(2,128)S(1)}, f32[2,256]{1,0:T(2,128)}, u32[]{:S(2)}) copy-start(f32[2,256]{1,0:T(2,128)} %fracs_two.1) | copy-start | bytes 6148
  1.3 0.7 %copy-start.2 = (bf16[2,512]{1,0:T(2,128)(2,1)S(1)}, bf16[2,512]{1,0:T(2,128)(2,1)}, u32[]{:S(2)}) copy-start(bf16[2,512]{1,0:T(2,128)(2,1)} %chirp_ref.1) | copy-start | bytes 6148
  1.3 0.7 %copy-start.3 = (s32[2,256]{1,0:T(2,128)S(1)}, s32[2,256]{1,0:T(2,128)}, u32[]{:S(2)}) copy-start(s32[2,256]{1,0:T(2,128)} %beam_two.1) | copy-start | bytes 6148
  1.3 0.7 %copy-start.4 = (s32[2,256]{1,0:T(2,128)S(1)}, s32[2,256]{1,0:T(2,128)}, u32[]{:S(2)}) copy-start(s32[2,256]{1,0:T(2,128)} %shift_two.1) | copy-start | bytes 6148
  1.3 0.7 %copy-start.5 = (f32[2,256]{1,0:T(2,128)S(1)}, f32[2,256]{1,0:T(2,128)}, u32[]{:S(2)}) copy-start(f32[2,256]{1,0:T(2,128)} %base_two.1) | copy-start | bytes 6148
  1.3 0.7 %copy-start.6 = (s32[2,128]{1,0:T(2,128)S(1)}, s32[2,128]{1,0:T(2,128)}, u32[]{:S(2)}) copy-start(s32[2,128]{1,0:T(2,128)} %beam_one.1) | copy-start | bytes 3076
  1.3 0.7 %copy-start.7 = (s32[2,128]{1,0:T(2,128)S(1)}, s32[2,128]{1,0:T(2,128)}, u32[]{:S(2)}) copy-start(s32[2,128]{1,0:T(2,128)} %shift_one.1) | copy-start | bytes 3076
  1.3 0.7 %copy-start.8 = (f32[2,128]{1,0:T(2,128)S(1)}, f32[2,128]{1,0:T(2,128)}, u32[]{:S(2)}) copy-start(f32[2,128]{1,0:T(2,128)} %base_one.1) | copy-start | bytes 3076
  1.5 0.7 %copy-start.1 = (f32[2,128]{1,0:T(2,128)S(1)}, f32[2,128]{1,0:T(2,128)}, u32[]{:S(2)}) copy-start(f32[2,128]{1,0:T(2,128)} %fracs_one.1) | copy-start | bytes 3076
